TPU v7x, 32 devices: a whole 2x2x4 slice. The times are simulated.
32 devices in a mesh: rows: 4 (over y, x), cols: 8 (over z, core).
Axes of the slice: x: 2, y: 2, z: 4, core: 2. Of those that a mesh axis runs over, the one named last changes fastest.
Arguments:
- power: float32 [2, 4, 512, 1024], P(None, None, 'rows', 'cols'), may hold values from -6 to 6
- material: int32 [4, 512, 1024], P(None, 'rows', 'cols'), may hold values from 0 to 7
- cond_table: float32 [4, 8], replicated, may hold values from 0.5 to 8
- tier_table: int32 [4], replicated, may hold values from 0 to 3
- coarse_slot: int32 [32], replicated, may hold values from 0 to 31, each once
- coarse_inverse: float32 [8, 4, 4], replicated, as said below
Outputs:
- solution: float32 [2, 4, 512, 1024], P(None, None, 'rows', 'cols')
- residual: float32 [2, 4, 512, 1024], P(None, None, 'rows', 'cols')
- precond: float32 [2, 4, 512, 1024], P(None, None, 'rows', 'cols')
Inputs may be any that keep to these rules, and one draw needn't show every extreme that they name: `coarse_slot`: each value once. `coarse_inverse`: symmetric within each owner.
All inputs are finite; a program needn't handle non-finite values.
Results may differ from a plain program's by a relative error of at most 0.0003.
Values sent between devices are 32-bit elements; how exact they have to be, the bound alone decides.
A program may use at most 64 MiB of HBM per device.

v0:
```python
import math

import jax
import jax.numpy as jnp
import numpy as np
from jax import lax
from jax.experimental import pallas as pl
from jax.experimental.pallas import tpu as pltpu
from jax.sharding import PartitionSpec as P

SUB = 128
HALF = SUB // 2
TIERS = 4
ITERS = 2

SHIFT_C = 0.5
VERT_C = 2.0
SINK_C = 0.05
MESH = pl.DeviceIdType.MESH


def split_constants():
    counting = np.arange(1, SUB + 1)
    angle = np.pi / (SUB + 1)
    product = (counting[:, None] * counting[None, :]) % (2 * (SUB + 1))
    basis = np.sqrt(2.0 / (SUB + 1)) * np.sin(angle * product)
    eigen = 2.0 - 2.0 * np.cos(angle * counting)
    recip = 1.0 / (eigen[:, None] + eigen[None, :] + SHIFT_C)
    rolled = np.roll(basis, HALF, axis=0)
    rights, lefts = [], []
    for matrix in (basis, rolled, rolled.T):
        high = matrix.astype(np.float32).astype(jnp.bfloat16)
        low = (matrix - high.astype(np.float64)).astype(np.float32).astype(jnp.bfloat16)
        wide = np.concatenate([high, low], 1)
        rights.append(np.concatenate([wide, wide], 0))
        tall = np.concatenate([high, low], 0)
        lefts.append(np.concatenate([tall, tall], 1))
    return np.stack(rights), np.stack(lefts), recip.astype(np.float32)


def halves(value):
    high = value.astype(jnp.bfloat16)
    low = (value - high.astype(jnp.float32)).astype(jnp.bfloat16)
    return high, low


def kernel(
    rows, cols, variants, owners, own,
    power, material, rights, lefts, recip, cond_table, tier_table, slots, inverse,
    sol, res, pre,
    inv_den, coef, upward, sink, held, image, held_image,
    fwd_send, fwd_recv, back_send, back_recv,
    row_send, row_recv, col_send, col_recv, gather_cols, gather_rows,
    send_sem, recv_sem,
):
    i, j = lax.axis_index("rows"), lax.axis_index("cols")
    not_first_row, not_last_row = i > 0, i < rows - 1
    not_first_col, not_last_col = j > 0, j < cols - 1
    up, down = jnp.maximum(i - 1, 0), jnp.minimum(i + 1, rows - 1)
    before, after = jnp.maximum(j - 1, 0), jnp.minimum(j + 1, cols - 1)
    scale = 1.0 / math.sqrt(SUB * SUB * TIERS)

    barrier = pltpu.get_barrier_semaphore()
    for step in range(1, cols):
        pl.semaphore_signal(
            barrier, 1, device_id=(i, lax.rem(j + step, cols)), device_id_type=MESH
        )
    for step in range(1, rows):
        pl.semaphore_signal(
            barrier, 1, device_id=(lax.rem(i + step, rows), j), device_id_type=MESH
        )
    to_front = jnp.logical_and(not_first_row, not_first_col)
    to_back = jnp.logical_and(not_last_row, not_last_col)

    @pl.when(to_front)
    def _():
        pl.semaphore_signal(barrier, 1, device_id=(up, before), device_id_type=MESH)

    @pl.when(to_back)
    def _():
        pl.semaphore_signal(barrier, 1, device_id=(down, after), device_id_type=MESH)

    fwd_route = (
        ((up, before), to_front, to_back),
        ((up, j), not_first_row, not_last_row),
        ((i, before), not_first_col, not_last_col),
    )
    back_route = (
        ((down, after), to_back, to_front),
        ((down, j), not_last_row, not_first_row),
        ((i, after), not_last_col, not_first_col),
    )
    quads = ((0, 0), (0, 1), (1, 0))
    counter = [0]
    pending = []

    def message(source, target, device, may_send):
        number = counter[0]
        counter[0] += 1
        copy = pltpu.make_async_remote_copy(
            source, target, send_sem.at[number], recv_sem.at[number],
            device_id=device, device_id_type=MESH,
        )
        if may_send is None:
            copy.start()
        else:
            pl.when(may_send)(lambda: copy.start())
        pending.append((copy, may_send))
        return copy

    def receive(copy, may_receive):
        if may_receive is None:
            copy.wait_recv()
        else:
            pl.when(may_receive)(lambda: copy.wait_recv())

    lane = lax.broadcasted_iota(jnp.int32, (HALF, SUB), 1)
    is_left = lane < HALF
    full_lane = lax.broadcasted_iota(jnp.int32, (SUB, SUB), 1)
    full_row = lax.broadcasted_iota(jnp.int32, (SUB, SUB), 0)
    tile_lane = lax.broadcasted_iota(jnp.int32, (8, SUB), 1)

    def swap(value):
        return pltpu.roll(value, HALF, 1)

    def send_quads(tiles, sender, receiver, route, apply, v):
        copies = []
        for q, (low, right) in enumerate(quads):
            span = slice(low * HALF, (low + 1) * HALF)
            for pair in range(TIERS // 2):
                first, second = tiles[pair][span], tiles[pair + TIERS // 2][span]
                if right:
                    packed = jnp.where(is_left, swap(first), second)
                else:
                    packed = jnp.where(is_left, first, swap(second))
                sender[apply, v, q, pair] = packed
            device, may_send, may_receive = route[q]
            copy = message(
                sender.at[apply, v, q], receiver.at[apply, v, q], device, may_send
            )
            copies.append((copy, may_receive))
        return copies

    def quad_halves(receiver, apply, v, t):
        pair, second = t % (TIERS // 2), t >= TIERS // 2
        top_left = receiver[apply, v, 0, pair]
        top_right = receiver[apply, v, 1, pair]
        low_left = receiver[apply, v, 2, pair]
        if second:
            top_left, low_left = swap(top_left), swap(low_left)
        else:
            top_right = swap(top_right)
        return jnp.where(is_left, top_left, top_right), low_left

    def right_mul(value, which):
        high, low = halves(value)
        wide = jnp.dot(
            jnp.concatenate([high, low], 1), rights[which], preferred_element_type=jnp.float32
        )
        return wide[:, :SUB] + wide[:, SUB:]

    def left_mul(value, which):
        high, low = halves(value)
        tall = jnp.dot(
            lefts[which], jnp.concatenate([high, low], 0), preferred_element_type=jnp.float32
        )
        return tall[:SUB] + tall[SUB:]

    def solve(tiles, plan):
        first = right_mul(jnp.concatenate(tiles, 0), plan[0])
        mid = []
        for t in range(TIERS):
            spectral = left_mul(first[t * SUB : (t + 1) * SUB], plan[1])
            mid.append(left_mul(spectral * inv_den[t], plan[2]))
        last = right_mul(jnp.concatenate(mid, 0), plan[3])
        return [last[t * SUB : (t + 1) * SUB] for t in range(TIERS)]

    def start_halo(number, tiles):
        west = jnp.zeros((SUB, SUB), jnp.float32)
        east = jnp.zeros((SUB, SUB), jnp.float32)
        for k, tile in enumerate(tiles):
            row_send[number, 0, k : k + 1, :] = tile[0:1]
            row_send[number, 1, k : k + 1, :] = tile[SUB - 1 : SUB]
            west = jnp.where(full_lane == k, pltpu.roll(tile, k, 1) if k else tile, west)
            east = jnp.where(full_lane == k, pltpu.roll(tile, k + 1, 1), east)
        col_send[number, 0] = west
        col_send[number, 1] = east
        return (
            (message(col_send.at[number, 0], col_recv.at[number, 1], (i, before), not_first_col), not_last_col),
            (message(col_send.at[number, 1], col_recv.at[number, 0], (i, after), not_last_col), not_first_col),
            (message(row_send.at[number, 0], row_recv.at[number, 1], (up, j), not_first_row), not_last_row),
            (message(row_send.at[number, 1], row_recv.at[number, 0], (down, j), not_last_row), not_first_row),
        )

    def neighbours(number, k, tile):
        north = jnp.where(full_row == 0, row_recv[number, 0, k : k + 1, :], pltpu.roll(tile, 1, 0))
        south = jnp.where(
            full_row == SUB - 1, row_recv[number, 1, k : k + 1, :], pltpu.roll(tile, SUB - 1, 0)
        )
        from_west = col_recv[number, 0]
        if k:
            from_west = pltpu.roll(from_west, SUB - k, 1)
        from_east = pltpu.roll(col_recv[number, 1], SUB - 1 - k, 1)
        west = jnp.where(full_lane == 0, from_west, pltpu.roll(tile, 1, 1))
        east = jnp.where(full_lane == SUB - 1, from_east, pltpu.roll(tile, SUB - 1, 1))
        return north, south, west, east

    def gather_start(number, parts):
        total = jnp.sum(jnp.concatenate(parts, 0), axis=1, keepdims=True)
        gather_cols[number, j] = jnp.broadcast_to(total, (8, SUB))
        return [
            message(
                gather_cols.at[number, j], gather_cols.at[number, j],
                (i, lax.rem(j + step, cols)), None,
            )
            for step in range(1, cols)
        ]

    def gather_middle(number, copies):
        for copy in copies:
            receive(copy, None)
        merged = jnp.zeros((8, SUB), jnp.float32)
        for c in range(cols):
            merged = jnp.where(tile_lane == c, gather_cols[number, c], merged)
        gather_rows[number, i] = merged
        return [
            message(
                gather_rows.at[number, i], gather_rows.at[number, i],
                (lax.rem(i + step, rows), j), None,
            )
            for step in range(1, rows)
        ]

    def gather_end(number, copies):
        for copy in copies:
            receive(copy, None)
        return [gather_rows[number, r] for r in range(rows)]

    conds = []
    for t in range(TIERS):
        table = tier_table[t]
        ids = material[t]
        cond = jnp.zeros((SUB, SUB), jnp.float32)
        mean = 0.0
        mats = cond_table.shape[1]
        for m in range(mats):
            entry = cond_table[table, m]
            mean = mean + entry
            cond = jnp.where(ids == m, entry, cond)
        conds.append(cond)
        inv_mean = 1.0 / (jnp.full((8, SUB), mean, jnp.float32) * (1.0 / mats))
        inv_den[t] = recip[...] * inv_mean[0:1]

    for q in range(3):
        for route, receiver in ((fwd_route, fwd_recv), (back_route, back_recv)):

            @pl.when(jnp.logical_not(route[q][2]))
            def _():
                for apply in range(ITERS + 1):
                    for v in range(variants):
                        receiver[apply, v, q] = jnp.zeros(receiver.shape[3:], jnp.float32)

    for side, has_row, has_col in ((0, not_first_row, not_first_col), (1, not_last_row, not_last_col)):

        @pl.when(jnp.logical_not(has_row))
        def _():
            for number in range(ITERS + 1):
                row_recv[number, side] = jnp.zeros((8, SUB), jnp.float32)

        @pl.when(jnp.logical_not(has_col))
        def _():
            for number in range(ITERS + 1):
                col_recv[number, side] = jnp.zeros((SUB, SUB), jnp.float32)

    pl.semaphore_wait(
        barrier,
        cols - 1 + rows - 1 + to_front.astype(jnp.int32) + to_back.astype(jnp.int32),
    )

    def tile_sum(values):
        return jnp.sum(values, axis=0, keepdims=True)

    def start_apply(apply, get):
        return [
            send_quads(get(v), fwd_send, fwd_recv, fwd_route, apply, v) for v in range(variants)
        ]

    def residual_of(v):
        return [res[v, t] for t in range(TIERS)]

    res[...] = power[...]
    forward = start_apply(0, residual_of)
    cond_halo = start_halo(0, conds)
    zero_row = jnp.zeros((1, SUB), jnp.float32)
    sums = [
        tile_sum(sum(residual_of(v)[1:], residual_of(v)[0])) * scale for v in range(variants)
    ]
    gather = gather_start(0, [zero_row] * 6 + sums)

    mine = slots[i * cols + j]
    my_owner, my_place = lax.div(mine, own), lax.rem(mine, own)
    weights = []
    row_lane = lax.broadcasted_iota(jnp.int32, (1, SUB), 1)
    for r in range(rows):
        line = zero_row
        for c in range(cols):
            other = slots[r * cols + c]
            entry = inverse[my_owner, my_place, lax.rem(other, own)]
            entry = jnp.where(lax.div(other, own) == my_owner, entry, 0.0)
            line = jnp.where(row_lane == c, entry, line)
        weights.append(line)

    gather = gather_middle(0, gather)

    def aligned(v):
        for t, tile in enumerate(solve(residual_of(v), (0, 0, 0, 0))):
            pre[v, t] = tile

    def coarse_of(coarse_state):
        mixed = weights[0] * coarse_state[0]
        for r in range(1, rows):
            mixed = mixed + weights[r] * coarse_state[r]
        return jnp.sum(mixed, axis=1, keepdims=True) * scale

    def finish_apply(apply, forward, get_coarse):
        for v in range(variants):
            aligned(v)
        backs = []
        for v in range(variants):
            for copy, may_receive in forward[v]:
                receive(copy, may_receive)
            frames = []
            for t in range(TIERS):
                top, low_left = quad_halves(fwd_recv, apply, v, t)
                low = jnp.where(is_left, low_left, res[v, t, HALF:, :])
                frames.append(jnp.concatenate([top, low], 0))
            solved = solve(frames, (1, 2, 1, 2))
            backs.append(send_quads(solved, back_send, back_recv, back_route, apply, v))
            for t in range(TIERS):
                keep = jnp.where(is_left, 0.0, solved[t][HALF:])
                pre[v, t, HALF:, :] = pre[v, t, HALF:, :] + keep
        coarse = get_coarse()
        for v in range(variants):
            shift = coarse[6 + v : 7 + v]
            for copy, may_receive in backs[v]:
                receive(copy, may_receive)
            for t in range(TIERS):
                top, low_left = quad_halves(back_recv, apply, v, t)
                pre[v, t, :HALF, :] = pre[v, t, :HALF, :] + top + shift
                low = jnp.where(is_left, low_left, 0.0)
                pre[v, t, HALF:, :] = pre[v, t, HALF:, :] + low + shift

    for copy, may_receive in cond_halo:
        receive(copy, may_receive)
    for t in range(TIERS):
        for side, other in enumerate(neighbours(0, t, conds[t])):
            coef[t, side] = 0.5 * (conds[t] + other)
        if t + 1 < TIERS:
            upward[t] = VERT_C * 0.5 * (conds[t] + conds[t + 1])
    sink[...] = SINK_C * conds[0]

    coarse_state = None

    def first_coarse():
        nonlocal coarse_state
        coarse_state = gather_end(0, gather)
        return coarse_of(coarse_state)

    finish_apply(0, forward, first_coarse)

    rz_old = curvature = coarse_image = None
    for number in range(ITERS):
        tiles = [[pre[v, t] for t in range(TIERS)] for v in range(variants)]
        halo = start_halo(number + 1, [tile for group in tiles for tile in group])
        for copy, may_receive in halo:
            receive(copy, may_receive)
        rz_parts, uw_parts, us_parts, q_parts = [], [], [], []
        for v in range(variants):
            rz_sum = uw_sum = us_sum = q_sum = zero_row
            for t in range(TIERS):
                tile = pre[v, t]
                out = None
                for side, other in enumerate(neighbours(number + 1, v * TIERS + t, tile)):
                    term = coef[t, side] * (tile - other)
                    out = term if out is None else out + term
                if t + 1 < TIERS:
                    out = out + upward[t] * (tile - pre[v, t + 1])
                if t:
                    out = out - upward[t - 1] * (pre[v, t - 1] - tile)
                else:
                    out = out + sink[...] * tile
                image[v, t] = out
                rz_sum = rz_sum + tile_sum(res[v, t] * tile)
                uw_sum = uw_sum + tile_sum(out * tile)
                q_sum = q_sum + tile_sum(out)
                if number:
                    us_sum = us_sum + tile_sum(held_image[v, t] * tile)
            rz_parts.append(rz_sum)
            uw_parts.append(uw_sum)
            us_parts.append(us_sum)
            q_parts.append(q_sum * scale)
        gather = gather_start(number + 1, rz_parts + uw_parts + us_parts + q_parts)
        gather = gather_middle(number + 1, gather)
        gathered = gather_end(number + 1, gather)
        total = gathered[0]
        for r in range(1, rows):
            total = total + gathered[r]
        total = jnp.broadcast_to(jnp.sum(total, axis=1, keepdims=True), (8, SUB))
        rz, uw, us = total[0:2], total[2:4], total[4:6]
        if number:
            beta = rz / rz_old
            curvature = uw + 2.0 * beta * us + beta * beta * curvature
        else:
            beta = None
            curvature = uw
        alpha = rz / curvature
        rz_old = rz

        last = []
        for v in range(variants):
            step = alpha[v : v + 1]
            residuals = []
            for t in range(TIERS):
                if number:
                    turn = beta[v : v + 1]
                    moved = image[v, t] + turn * held_image[v, t]
                else:
                    moved = image[v, t]
                if number + 1 < ITERS:
                    held_image[v, t] = moved
                updated = res[v, t] - step * moved
                res[v, t] = updated
                residuals.append(updated)
            last.append(
                send_quads(residuals, fwd_send, fwd_recv, fwd_route, number + 1, v)
            )
        for v in range(variants):
            step = alpha[v : v + 1]
            for t in range(TIERS):
                if number:
                    heading = pre[v, t] + beta[v : v + 1] * held[v, t]
                    sol[v, t] = sol[v, t] + step * heading
                else:
                    heading = pre[v, t]
                    sol[v, t] = step * heading
                if number + 1 < ITERS:
                    held[v, t] = heading

        wide_alpha = jnp.concatenate([alpha] * 4, 0)
        if number:
            wide_beta = jnp.concatenate([beta] * 4, 0)
            coarse_image = [g + wide_beta * c for g, c in zip(gathered, coarse_image)]
        else:
            coarse_image = gathered
        coarse_state = [q - wide_alpha * c for q, c in zip(coarse_state, coarse_image)]
        finish_apply(number + 1, last, lambda: coarse_of(coarse_state))

    for copy, may_send in pending:
        if may_send is None:
            copy.wait_send()
        else:
            pl.when(may_send)(lambda copy=copy: copy.wait_send())


def solution(mesh):
    rows, cols = mesh.shape["rows"], mesh.shape["cols"]
    rights, lefts, recip = split_constants()

    def shards(power, material, cond_table, tier_table, coarse_slot, coarse_inverse):
        variants = power.shape[0]
        owners, own = coarse_inverse.shape[:2]
        applies = ITERS + 1
        messages = applies * variants * 6 + applies * 4 + applies * (rows - 1 + cols - 1)
        vmem = pl.BlockSpec(memory_space=pltpu.VMEM)
        smem = pl.BlockSpec(memory_space=pltpu.SMEM)
        field = (variants, TIERS, SUB, SUB)
        quad = (applies, variants, 3, TIERS // 2, HALF, SUB)

        def body(*refs):
            kernel(rows, cols, variants, owners, own, *refs)

        f32 = jnp.float32
        return pl.pallas_call(
            body,
            out_shape=[jax.ShapeDtypeStruct(power.shape, f32)] * 3,
            in_specs=[vmem] * 5 + [smem] * 4,
            out_specs=[vmem] * 3,
            scratch_shapes=[
                pltpu.VMEM((TIERS, SUB, SUB), f32),
                pltpu.VMEM((TIERS, 4, SUB, SUB), f32),
                pltpu.VMEM((TIERS - 1, SUB, SUB), f32),
                pltpu.VMEM((SUB, SUB), f32),
                pltpu.VMEM(field, f32),
                pltpu.VMEM(field, f32),
                pltpu.VMEM(field, f32),
                pltpu.VMEM(quad, f32),
                pltpu.VMEM(quad, f32),
                pltpu.VMEM(quad, f32),
                pltpu.VMEM(quad, f32),
                pltpu.VMEM((applies, 2, 8, SUB), f32),
                pltpu.VMEM((applies, 2, 8, SUB), f32),
                pltpu.VMEM((applies, 2, SUB, SUB), f32),
                pltpu.VMEM((applies, 2, SUB, SUB), f32),
                pltpu.VMEM((applies, cols, 8, SUB), f32),
                pltpu.VMEM((applies, rows, 8, SUB), f32),
                pltpu.SemaphoreType.DMA((messages,)),
                pltpu.SemaphoreType.DMA((messages,)),
            ],
            compiler_params=pltpu.CompilerParams(
                collective_id=0, has_side_effects=True, vmem_limit_bytes=48 * 1024 * 1024
            ),
        )(
            power, material, jnp.asarray(rights), jnp.asarray(lefts), jnp.asarray(recip),
            cond_table, tier_table, coarse_slot, coarse_inverse,
        )

    in_specs = (P(None, None, "rows", "cols"), P(None, "rows", "cols"), P(), P(), P(), P())
    out_specs = (P(None, None, "rows", "cols"),) * 3
    return jax.shard_map(shards, mesh=mesh, in_specs=in_specs, out_specs=out_specs, check_vma=False)
```

profile of v0, /device:TPU:12, one launch (start us, length us, event | category | flops | bytes accessed | tf_op | source)
XLA Modules:
  0.0 80.9 jit_solution(17823503193973067199)
XLA Ops:
  0.6 0.0 copy-start.7
  0.6 0.0 copy-start.6
  0.7 0.0 copy-start.5
  0.7 0.8 %copy.12.refs_8_ = f32[8,4,4]{2,1,0:T(4,128)S(1)} copy(f32[8,4,4]{0,2,1:T(4,128)} %param.14) | data formatting | bytes 1024 | tf_op args[5]
  1.5 0.0 copy-done.7
  1.5 0.0 copy-done.6
  1.5 0.0 copy-done.5
  1.5 0.0 copy-start
  1.5 1.0 %copy-done = f32[2,4,128,128]{3,2,1,0:T(8,128)S(1)} copy-done((f32[2,4,128,128]{3,2,1,0:T(8,128)S(1)}, f32[2,4,128,128]{3,2,1,0:T(8,128)}, u32[]{:S(2)}) %copy-start) | copy-done | bytes 524312
  2.5 0.0 copy-start.1
  2.5 1.0 %copy-done.1 = bf16[3,256,256]{2,1,0:T(8,128)(2,1)S(1)} copy-done((bf16[3,256,256]{2,1,0:T(8,128)(2,1)S(1)}, bf16[3,256,256]{2,1,0:T(8,128)(2,1)}, u32[]{:S(2)}) %copy-start.1) | copy-done | bytes 393240
  3.5 0.0 copy-start.2
  3.5 1.0 %copy-done.2 = bf16[3,256,256]{2,1,0:T(8,128)(2,1)S(1)} copy-done((bf16[3,256,256]{2,1,0:T(8,128)(2,1)S(1)}, bf16[3,256,256]{2,1,0:T(8,128)(2,1)}, u32[]{:S(2)}) %copy-start.2) | copy-done | bytes 393240
  4.5 0.0 copy-start.3
  4.5 0.9 %copy-done.3 = s32[4,128,128]{2,1,0:T(8,128)S(1)} copy-done((s32[4,128,128]{2,1,0:T(8,128)S(1)}, s32[4,128,128]{2,1,0:T(8,128)}, u32[]{:S(2)}) %copy-start.3) | copy-done | bytes 262168
  5.5 0.0 copy-start.4
  5.5 0.8 %copy-done.4 = f32[128,128]{1,0:T(8,128)S(1)} copy-done((f32[128,128]{1,0:T(8,128)S(1)}, f32[128,128]{1,0:T(8,128)}, u32[]{:S(2)}) %copy-start.4) | copy-done | bytes 65560
  6.3 72.2 %shard_map.112 = (f32[2,4,128,128]{3,2,1,0:T(8,128)S(1)}, f32[2,4,128,128]{3,2,1,0:T(8,128)S(1)}, f32[2,4,128,128]{3,2,1,0:T(8,128)S(1)}) custom-call(f32[2,4,128,128]{3,2,1,0:T(8,128)S(1)} %copy-done, s32[4,128,128]{2,1,0:T(8,128)S(1)} %copy-done.3, bf16[3,256,256]{2,1,0:T(8,128)(2,1)S(1)} %copy-done.2, bf16[3,256,256]{2,1,0:T(8,128)(2,1)S(1)} %copy-done.1, ...), custom_call_target="tpu_custom_call" | custom-call | tf_op jit(solution)/shard_map/pallas_call | solution.py:483
  78.5 0.8 copy.16
  79.3 0.8 copy.17
  80.1 0.8 copy.18
Async XLA Ops:
  0.6 0.8 %copy-start.7 = (s32[32]{0:T(128)S(1)}, s32[32]{0:T(128)}, u32[]{:S(2)}) copy-start(s32[32]{0:T(128)} %refs_7_.1) | copy-start | bytes 388
  0.6 0.8 %copy-start.6 = (s32[4]{0:T(128)S(1)}, s32[4]{0:T(128)}, u32[]{:S(2)}) copy-start(s32[4]{0:T(128)} %refs_6_.1) | copy-start | bytes 52
  0.7 0.8 %copy-start.5 = (f32[4,8]{1,0:T(4,128)S(1)}, f32[4,8]{1,0:T(4,128)}, u32[]{:S(2)}) copy-start(f32[4,8]{1,0:T(4,128)} %refs_5_.1) | copy-start | bytes 388
  1.5 1.0 %copy-start = (f32[2,4,128,128]{3,2,1,0:T(8,128)S(1)}, f32[2,4,128,128]{3,2,1,0:T(8,128)}, u32[]{:S(2)}) copy-start(f32[2,4,128,128]{3,2,1,0:T(8,128)} %refs_0_.1) | copy-start | bytes 1572868
  2.5 1.0 %copy-start.1 = (bf16[3,256,256]{2,1,0:T(8,128)(2,1)S(1)}, bf16[3,256,256]{2,1,0:T(8,128)(2,1)}, u32[]{:S(2)}) copy-start(bf16[3,256,256]{2,1,0:T(8,128)(2,1)} %constant.7.clone.refs_3_) | copy-start | bytes 1179652
  3.5 1.0 %copy-start.2 = (bf16[3,256,256]{2,1,0:T(8,128)(2,1)S(1)}, bf16[3,256,256]{2,1,0:T(8,128)(2,1)}, u32[]{:S(2)}) copy-start(bf16[3,256,256]{2,1,0:T(8,128)(2,1)} %constant.6.clone.refs_2_) | copy-start | bytes 1179652
  4.5 0.9 %copy-start.3 = (s32[4,128,128]{2,1,0:T(8,128)S(1)}, s32[4,128,128]{2,1,0:T(8,128)}, u32[]{:S(2)}) copy-start(s32[4,128,128]{2,1,0:T(8,128)} %refs_1_.1) | copy-start | bytes 786436
  5.5 0.8 %copy-start.4 = (f32[128,128]{1,0:T(8,128)S(1)}, f32[128,128]{1,0:T(8,128)}, u32[]{:S(2)}) copy-start(f32[128,128]{1,0:T(8,128)} %constant.8.clone.refs_4_) | copy-start | bytes 196612
where the time goes:
time: 81.5 us; the launch traced here: 80.9 us
  Pallas kernels  72.2 us (89%)
  local copies, waits for them, and re-layouts  8.02 us (10%)
    pallas_call x1, Pallas kernels, shards(): pl.pallas_call(body, out_shape=[jax.ShapeDtypeStruct(power.shape, f32)] *...  72.2 us
    unnamed x20, local copies, waits for them, and re-layouts  8.02 us

commit v1 on v0

--- a/solution.py
+++ b/solution.py
@@ -46,13 +46,24 @@
 
 def kernel(
     rows, cols, variants, owners, own,
-    power, material, rights, lefts, recip, cond_table, tier_table, slots, inverse,
-    sol, res, pre,
+    power_hbm, material_hbm, rights_hbm, lefts_hbm, recip_hbm, inverse_hbm,
+    cond_table, tier_table, slots,
+    sol_hbm, res_hbm, pre_hbm,
+    sol, res, pre, material, rights, lefts, recip, inverse, frame_res, frame_image,
     inv_den, coef, upward, sink, held, image, held_image,
     fwd_send, fwd_recv, back_send, back_recv,
     row_send, row_recv, col_send, col_recv, gather_cols, gather_rows,
-    send_sem, recv_sem,
+    send_sem, recv_sem, load_sem,
 ):
+    loads = [
+        pltpu.make_async_copy(source, target, load_sem.at[number])
+        for number, (source, target) in enumerate((
+            (material_hbm, material), (power_hbm, res), (recip_hbm, recip),
+            (rights_hbm, rights), (lefts_hbm, lefts), (inverse_hbm, inverse),
+        ))
+    ]
+    for load in loads:
+        load.start()
     i, j = lax.axis_index("rows"), lax.axis_index("cols")
     not_first_row, not_last_row = i > 0, i < rows - 1
     not_first_col, not_last_col = j > 0, j < cols - 1
@@ -236,6 +247,9 @@
             receive(copy, None)
         return [gather_rows[number, r] for r in range(rows)]
 
+    for load in loads[:3]:
+        load.wait()
+
     conds = []
     for t in range(TIERS):
         table = tier_table[t]
@@ -264,12 +278,12 @@
 
         @pl.when(jnp.logical_not(has_row))
         def _():
-            for number in range(ITERS + 1):
+            for number in range(ITERS * variants + 1):
                 row_recv[number, side] = jnp.zeros((8, SUB), jnp.float32)
 
         @pl.when(jnp.logical_not(has_col))
         def _():
-            for number in range(ITERS + 1):
+            for number in range(ITERS * variants + 1):
                 col_recv[number, side] = jnp.zeros((SUB, SUB), jnp.float32)
 
     pl.semaphore_wait(
@@ -288,7 +302,6 @@
     def residual_of(v):
         return [res[v, t] for t in range(TIERS)]
 
-    res[...] = power[...]
     forward = start_apply(0, residual_of)
     cond_halo = start_halo(0, conds)
     zero_row = jnp.zeros((1, SUB), jnp.float32)
@@ -297,24 +310,25 @@
     ]
     gather = gather_start(0, [zero_row] * 6 + sums)
 
+    for load in loads[3:]:
+        load.wait()
     mine = slots[i * cols + j]
     my_owner, my_place = lax.div(mine, own), lax.rem(mine, own)
+    block = inverse[my_place]
+    owner_lane = lax.broadcasted_iota(jnp.int32, block.shape, 1)
+    entries = jnp.sum(jnp.where(owner_lane == my_owner, block, 0.0), axis=1, keepdims=True)
     weights = []
     row_lane = lax.broadcasted_iota(jnp.int32, (1, SUB), 1)
     for r in range(rows):
+        places = jnp.full((1, SUB), -1, jnp.int32)
+        for c in range(cols):
+            places = jnp.where(row_lane == c, slots[r * cols + c] - my_owner * own, places)
         line = zero_row
-        for c in range(cols):
-            other = slots[r * cols + c]
-            entry = inverse[my_owner, my_place, lax.rem(other, own)]
-            entry = jnp.where(lax.div(other, own) == my_owner, entry, 0.0)
-            line = jnp.where(row_lane == c, entry, line)
+        for k in range(own):
+            line = jnp.where(places == k, entries[k : k + 1], line)
         weights.append(line)
 
     gather = gather_middle(0, gather)
-
-    def aligned(v):
-        for t, tile in enumerate(solve(residual_of(v), (0, 0, 0, 0))):
-            pre[v, t] = tile
 
     def coarse_of(coarse_state):
         mixed = weights[0] * coarse_state[0]
@@ -322,9 +336,7 @@
             mixed = mixed + weights[r] * coarse_state[r]
         return jnp.sum(mixed, axis=1, keepdims=True) * scale
 
-    def finish_apply(apply, forward, get_coarse):
-        for v in range(variants):
-            aligned(v)
+    def solve_frames(apply, forward, own_low, update):
         backs = []
         for v in range(variants):
             for copy, may_receive in forward[v]:
@@ -332,23 +344,47 @@
             frames = []
             for t in range(TIERS):
                 top, low_left = quad_halves(fwd_recv, apply, v, t)
-                low = jnp.where(is_left, low_left, res[v, t, HALF:, :])
-                frames.append(jnp.concatenate([top, low], 0))
+                low = jnp.where(is_left, low_left, own_low[v, t, HALF:, :])
+                frames.append(update(v, t, jnp.concatenate([top, low], 0)))
             solved = solve(frames, (1, 2, 1, 2))
             backs.append(send_quads(solved, back_send, back_recv, back_route, apply, v))
             for t in range(TIERS):
-                keep = jnp.where(is_left, 0.0, solved[t][HALF:])
-                pre[v, t, HALF:, :] = pre[v, t, HALF:, :] + keep
-        coarse = get_coarse()
+                pre[v, t, HALF:, :] = jnp.where(is_left, 0.0, solved[t][HALF:])
+        return backs
+
+    def add_aligned(v, coarse):
+        shift = coarse[6 + v : 7 + v]
+        for t, tile in enumerate(solve(residual_of(v), (0, 0, 0, 0))):
+            pre[v, t, :HALF, :] = tile[:HALF] + shift
+            pre[v, t, HALF:, :] = pre[v, t, HALF:, :] + tile[HALF:] + shift
+
+    def add_offset(apply, backs, v):
+        for copy, may_receive in backs[v]:
+            receive(copy, may_receive)
+        for t in range(TIERS):
+            top, low_left = quad_halves(back_recv, apply, v, t)
+            pre[v, t, :HALF, :] = pre[v, t, :HALF, :] + top
+            low = jnp.where(is_left, low_left, 0.0)
+            pre[v, t, HALF:, :] = pre[v, t, HALF:, :] + low
+
+    def halo_of(number, v):
+        return 1 + number * variants + v
+
+    def finish_apply(apply, backs, coarse):
+        halos = []
         for v in range(variants):
-            shift = coarse[6 + v : 7 + v]
-            for copy, may_receive in backs[v]:
-                receive(copy, may_receive)
-            for t in range(TIERS):
-                top, low_left = quad_halves(back_recv, apply, v, t)
-                pre[v, t, :HALF, :] = pre[v, t, :HALF, :] + top + shift
-                low = jnp.where(is_left, low_left, 0.0)
-                pre[v, t, HALF:, :] = pre[v, t, HALF:, :] + low + shift
+            add_aligned(v, coarse)
+        for v in range(variants):
+            add_offset(apply, backs, v)
+            if apply < ITERS:
+                halos.append(start_halo(halo_of(apply, v), [pre[v, t] for t in range(TIERS)]))
+            else:
+                store = pltpu.make_async_copy(
+                    pre.at[v], pre_hbm.at[v], load_sem.at[len(loads) + 2 + v]
+                )
+                store.start()
+                halos.append(store)
+        return halos
 
     for copy, may_receive in cond_halo:
         receive(copy, may_receive)
@@ -359,28 +395,26 @@
             upward[t] = VERT_C * 0.5 * (conds[t] + conds[t + 1])
     sink[...] = SINK_C * conds[0]
 
-    coarse_state = None
-
-    def first_coarse():
-        nonlocal coarse_state
-        coarse_state = gather_end(0, gather)
-        return coarse_of(coarse_state)
-
-    finish_apply(0, forward, first_coarse)
+    def keep_frame(v, t, frame):
+        frame_res[v, t] = frame
+        return frame
+
+    backs = solve_frames(0, forward, res, keep_frame)
+    coarse_state = gather_end(0, gather)
+    halos = finish_apply(0, backs, coarse_of(coarse_state))
 
     rz_old = curvature = coarse_image = None
     for number in range(ITERS):
-        tiles = [[pre[v, t] for t in range(TIERS)] for v in range(variants)]
-        halo = start_halo(number + 1, [tile for group in tiles for tile in group])
-        for copy, may_receive in halo:
-            receive(copy, may_receive)
-        rz_parts, uw_parts, us_parts, q_parts = [], [], [], []
-        for v in range(variants):
+        rz_parts, uw_parts, us_parts, q_parts, forward = [], [], [], [], []
+
+        def apply_operator(v):
+            for copy, may_receive in halos[v]:
+                receive(copy, may_receive)
             rz_sum = uw_sum = us_sum = q_sum = zero_row
             for t in range(TIERS):
                 tile = pre[v, t]
                 out = None
-                for side, other in enumerate(neighbours(number + 1, v * TIERS + t, tile)):
+                for side, other in enumerate(neighbours(halo_of(number, v), t, tile)):
                     term = coef[t, side] * (tile - other)
                     out = term if out is None else out + term
                 if t + 1 < TIERS:
@@ -399,7 +433,21 @@
             uw_parts.append(uw_sum)
             us_parts.append(us_sum)
             q_parts.append(q_sum * scale)
+
+        def send_image(v):
+            forward.append(
+                send_quads(
+                    [image[v, t] for t in range(TIERS)],
+                    fwd_send, fwd_recv, fwd_route, number + 1, v,
+                )
+            )
+
+        for v in range(variants):
+            if v:
+                send_image(v - 1)
+            apply_operator(v)
         gather = gather_start(number + 1, rz_parts + uw_parts + us_parts + q_parts)
+        send_image(variants - 1)
         gather = gather_middle(number + 1, gather)
         gathered = gather_end(number + 1, gather)
         total = gathered[0]
@@ -416,24 +464,16 @@
         alpha = rz / curvature
         rz_old = rz
 
-        last = []
-        for v in range(variants):
-            step = alpha[v : v + 1]
-            residuals = []
-            for t in range(TIERS):
-                if number:
-                    turn = beta[v : v + 1]
-                    moved = image[v, t] + turn * held_image[v, t]
-                else:
-                    moved = image[v, t]
-                if number + 1 < ITERS:
-                    held_image[v, t] = moved
-                updated = res[v, t] - step * moved
-                res[v, t] = updated
-                residuals.append(updated)
-            last.append(
-                send_quads(residuals, fwd_send, fwd_recv, fwd_route, number + 1, v)
-            )
+        def update_frame(v, t, frame):
+            if number:
+                frame = frame + beta[v : v + 1] * frame_image[v, t]
+            if number + 1 < ITERS:
+                frame_image[v, t] = frame
+            updated = frame_res[v, t] - alpha[v : v + 1] * frame
+            if number + 1 < ITERS:
+                frame_res[v, t] = updated
+            return updated
+
         for v in range(variants):
             step = alpha[v : v + 1]
             for t in range(TIERS):
@@ -445,6 +485,16 @@
                     sol[v, t] = step * heading
                 if number + 1 < ITERS:
                     held[v, t] = heading
+        backs = solve_frames(number + 1, forward, image, update_frame)
+        for v in range(variants):
+            step = alpha[v : v + 1]
+            for t in range(TIERS):
+                moved = image[v, t]
+                if number:
+                    moved = moved + beta[v : v + 1] * held_image[v, t]
+                if number + 1 < ITERS:
+                    held_image[v, t] = moved
+                res[v, t] = res[v, t] - step * moved
 
         wide_alpha = jnp.concatenate([alpha] * 4, 0)
         if number:
@@ -453,8 +503,17 @@
         else:
             coarse_image = gathered
         coarse_state = [q - wide_alpha * c for q, c in zip(coarse_state, coarse_image)]
-        finish_apply(number + 1, last, lambda: coarse_of(coarse_state))
-
+        if number + 1 == ITERS:
+            stores = [
+                pltpu.make_async_copy(sol, sol_hbm, load_sem.at[len(loads)]),
+                pltpu.make_async_copy(res, res_hbm, load_sem.at[len(loads) + 1]),
+            ]
+            for store in stores:
+                store.start()
+        halos = finish_apply(number + 1, backs, coarse_of(coarse_state))
+
+    for store in stores + halos:
+        store.wait()
     for copy, may_send in pending:
         if may_send is None:
             copy.wait_send()
@@ -462,6 +521,19 @@
             pl.when(may_send)(lambda copy=copy: copy.wait_send())
 
 
+def write_out(*refs):
+    count = len(refs) // 2
+    sources, targets, sem = refs[:count], refs[count : 2 * count], refs[-1]
+    copies = [
+        pltpu.make_async_copy(source, target, sem.at[number])
+        for number, (source, target) in enumerate(zip(sources, targets))
+    ]
+    for copy in copies:
+        copy.start()
+    for copy in copies:
+        copy.wait()
+
+
 def solution(mesh):
     rows, cols = mesh.shape["rows"], mesh.shape["cols"]
     rights, lefts, recip = split_constants()
@@ -470,8 +542,9 @@
         variants = power.shape[0]
         owners, own = coarse_inverse.shape[:2]
         applies = ITERS + 1
-        messages = applies * variants * 6 + applies * 4 + applies * (rows - 1 + cols - 1)
-        vmem = pl.BlockSpec(memory_space=pltpu.VMEM)
+        halos = ITERS * variants + 1
+        messages = applies * variants * 6 + halos * 4 + applies * (rows - 1 + cols - 1)
+        hbm = pl.BlockSpec(memory_space=pltpu.HBM)
         smem = pl.BlockSpec(memory_space=pltpu.SMEM)
         field = (variants, TIERS, SUB, SUB)
         quad = (applies, variants, 3, TIERS // 2, HALF, SUB)
@@ -480,12 +553,22 @@
             kernel(rows, cols, variants, owners, own, *refs)
 
         f32 = jnp.float32
-        return pl.pallas_call(
+        done = pl.pallas_call(
             body,
             out_shape=[jax.ShapeDtypeStruct(power.shape, f32)] * 3,
-            in_specs=[vmem] * 5 + [smem] * 4,
-            out_specs=[vmem] * 3,
+            in_specs=[hbm] * 6 + [smem] * 3,
+            out_specs=[hbm] * 3,
             scratch_shapes=[
+                pltpu.VMEM(field, f32),
+                pltpu.VMEM(field, f32),
+                pltpu.VMEM(field, f32),
+                pltpu.VMEM((TIERS, SUB, SUB), jnp.int32),
+                pltpu.VMEM(rights.shape, jnp.bfloat16),
+                pltpu.VMEM(lefts.shape, jnp.bfloat16),
+                pltpu.VMEM((SUB, SUB), f32),
+                pltpu.VMEM((own, own, owners), f32),
+                pltpu.VMEM(field, f32),
+                pltpu.VMEM(field, f32),
                 pltpu.VMEM((TIERS, SUB, SUB), f32),
                 pltpu.VMEM((TIERS, 4, SUB, SUB), f32),
                 pltpu.VMEM((TIERS - 1, SUB, SUB), f32),
@@ -497,22 +580,31 @@
                 pltpu.VMEM(quad, f32),
                 pltpu.VMEM(quad, f32),
                 pltpu.VMEM(quad, f32),
-                pltpu.VMEM((applies, 2, 8, SUB), f32),
-                pltpu.VMEM((applies, 2, 8, SUB), f32),
-                pltpu.VMEM((applies, 2, SUB, SUB), f32),
-                pltpu.VMEM((applies, 2, SUB, SUB), f32),
+                pltpu.VMEM((halos, 2, 8, SUB), f32),
+                pltpu.VMEM((halos, 2, 8, SUB), f32),
+                pltpu.VMEM((halos, 2, SUB, SUB), f32),
+                pltpu.VMEM((halos, 2, SUB, SUB), f32),
                 pltpu.VMEM((applies, cols, 8, SUB), f32),
                 pltpu.VMEM((applies, rows, 8, SUB), f32),
                 pltpu.SemaphoreType.DMA((messages,)),
                 pltpu.SemaphoreType.DMA((messages,)),
+                pltpu.SemaphoreType.DMA((8 + variants,)),
             ],
             compiler_params=pltpu.CompilerParams(
-                collective_id=0, has_side_effects=True, vmem_limit_bytes=48 * 1024 * 1024
+                collective_id=0, has_side_effects=True, vmem_limit_bytes=60 * 1024 * 1024
             ),
         )(
             power, material, jnp.asarray(rights), jnp.asarray(lefts), jnp.asarray(recip),
-            cond_table, tier_table, coarse_slot, coarse_inverse,
-        )
+            jnp.transpose(coarse_inverse, (1, 2, 0)), cond_table, tier_table, coarse_slot,
+        )
+        return pl.pallas_call(
+            write_out,
+            out_shape=[jax.ShapeDtypeStruct(power.shape, f32)] * 3,
+            in_specs=[hbm] * 3,
+            out_specs=[hbm] * 3,
+            scratch_shapes=[pltpu.SemaphoreType.DMA((3,))],
+            compiler_params=pltpu.CompilerParams(vmem_limit_bytes=60 * 1024 * 1024),
+        )(*done)
 
     in_specs = (P(None, None, "rows", "cols"), P(None, "rows", "cols"), P(), P(), P(), P())
     out_specs = (P(None, None, "rows", "cols"),) * 3

time: 81.5 us -> 110 us (1.35)
  Pallas kernels: 72.2 us -> 110 us
  local copies, waits for them, and re-layouts: 8.02 us -> 0 us
    pallas_call x0 -> x1, Pallas kernels: none -> 48.8 us  [shards(): pl.pallas_call(write_out, out_shape=[jax.ShapeDtypeStruct(power.shape, f3...]
    pallas_call x1, Pallas kernels: 72.2 us -> 60.8 us  [shards(): pl.pallas_call(body, out_shape=[jax.ShapeDtypeStruct(power.shape, f32)] *...]
    unnamed x20 -> x0, local copies, waits for them, and re-layouts: 8.02 us -> none
where the time goes in v1:
time: 110 us
  Pallas kernels  110 us (100%)
    pallas_call x1, Pallas kernels, shards(): pl.pallas_call(body, out_shape=[jax.ShapeDtypeStruct(power.shape, f32)] *...  60.8 us
    pallas_call x1, Pallas kernels, shards(): pl.pallas_call(write_out, out_shape=[jax.ShapeDtypeStruct(power.shape, f3...  48.8 us

profile of v1, /device:TPU:12, one launch (start us, length us, event | category | flops | bytes accessed | tf_op | source)
XLA Modules:
  0.0 110.2 jit_solution(5468201394409699091)
XLA Ops:
  0.6 60.8 %shard_map.112 = (f32[2,4,128,128]{3,2,1,0:T(8,128)}, f32[2,4,128,128]{3,2,1,0:T(8,128)}, f32[2,4,128,128]{3,2,1,0:T(8,128)}) custom-call(f32[2,4,128,128]{3,2,1,0:T(8,128)} %refs_0_.1, s32[4,128,128]{2,1,0:T(8,128)} %refs_1_.1, bf16[3,256,256]{2,1,0:T(8,128)(2,1)} %constant.6.clone.refs_2_, bf16[3,256,256]{2,1,0:T(8,128)(2,1)} %constant.7.clone.refs_3_, ...), custom_call_target="tpu_custom_call" | custom-call | tf_op jit(solution)/shard_map/pallas_call | solution.py:556
  61.4 48.8 %shard_map.113 = (f32[2,4,128,128]{3,2,1,0:T(8,128)}, f32[2,4,128,128]{3,2,1,0:T(8,128)}, f32[2,4,128,128]{3,2,1,0:T(8,128)}) custom-call(f32[2,4,128,128]{3,2,1,0:T(8,128)} %get-tuple-element.6.refs_0_, f32[2,4,128,128]{3,2,1,0:T(8,128)} %get-tuple-element.7.refs_1_, f32[2,4,128,128]{3,2,1,0:T(8,128)} %get-tuple-element.8.refs_2_), custom_call_target="tpu_custom_call" | custom-call | tf_op jit(solution)/shard_map/pallas_call | solution.py:600

commit v2 on v1

--- a/solution.py
+++ b/solution.py
@@ -48,7 +48,6 @@
     rows, cols, variants, owners, own,
     power_hbm, material_hbm, rights_hbm, lefts_hbm, recip_hbm, inverse_hbm,
     cond_table, tier_table, slots,
-    sol_hbm, res_hbm, pre_hbm,
     sol, res, pre, material, rights, lefts, recip, inverse, frame_res, frame_image,
     inv_den, coef, upward, sink, held, image, held_image,
     fwd_send, fwd_recv, back_send, back_recv,
@@ -378,12 +377,6 @@
             add_offset(apply, backs, v)
             if apply < ITERS:
                 halos.append(start_halo(halo_of(apply, v), [pre[v, t] for t in range(TIERS)]))
-            else:
-                store = pltpu.make_async_copy(
-                    pre.at[v], pre_hbm.at[v], load_sem.at[len(loads) + 2 + v]
-                )
-                store.start()
-                halos.append(store)
         return halos
 
     for copy, may_receive in cond_halo:
@@ -503,17 +496,8 @@
         else:
             coarse_image = gathered
         coarse_state = [q - wide_alpha * c for q, c in zip(coarse_state, coarse_image)]
-        if number + 1 == ITERS:
-            stores = [
-                pltpu.make_async_copy(sol, sol_hbm, load_sem.at[len(loads)]),
-                pltpu.make_async_copy(res, res_hbm, load_sem.at[len(loads) + 1]),
-            ]
-            for store in stores:
-                store.start()
         halos = finish_apply(number + 1, backs, coarse_of(coarse_state))
 
-    for store in stores + halos:
-        store.wait()
     for copy, may_send in pending:
         if may_send is None:
             copy.wait_send()
@@ -545,6 +529,7 @@
         halos = ITERS * variants + 1
         messages = applies * variants * 6 + halos * 4 + applies * (rows - 1 + cols - 1)
         hbm = pl.BlockSpec(memory_space=pltpu.HBM)
+        vmem = pl.BlockSpec(memory_space=pltpu.VMEM)
         smem = pl.BlockSpec(memory_space=pltpu.SMEM)
         field = (variants, TIERS, SUB, SUB)
         quad = (applies, variants, 3, TIERS // 2, HALF, SUB)
@@ -555,13 +540,10 @@
         f32 = jnp.float32
         done = pl.pallas_call(
             body,
-            out_shape=[jax.ShapeDtypeStruct(power.shape, f32)] * 3,
+            out_shape=[pltpu.VMEM(power.shape, f32)] * 3,
             in_specs=[hbm] * 6 + [smem] * 3,
-            out_specs=[hbm] * 3,
+            out_specs=[vmem] * 3,
             scratch_shapes=[
-                pltpu.VMEM(field, f32),
-                pltpu.VMEM(field, f32),
-                pltpu.VMEM(field, f32),
                 pltpu.VMEM((TIERS, SUB, SUB), jnp.int32),
                 pltpu.VMEM(rights.shape, jnp.bfloat16),
                 pltpu.VMEM(lefts.shape, jnp.bfloat16),
@@ -588,10 +570,10 @@
                 pltpu.VMEM((applies, rows, 8, SUB), f32),
                 pltpu.SemaphoreType.DMA((messages,)),
                 pltpu.SemaphoreType.DMA((messages,)),
-                pltpu.SemaphoreType.DMA((8 + variants,)),
+                pltpu.SemaphoreType.DMA((6,)),
             ],
             compiler_params=pltpu.CompilerParams(
-                collective_id=0, has_side_effects=True, vmem_limit_bytes=60 * 1024 * 1024
+                collective_id=0, has_side_effects=True, vmem_limit_bytes=58 * 1024 * 1024
             ),
         )(
             power, material, jnp.asarray(rights), jnp.asarray(lefts), jnp.asarray(recip),
@@ -600,10 +582,10 @@
         return pl.pallas_call(
             write_out,
             out_shape=[jax.ShapeDtypeStruct(power.shape, f32)] * 3,
-            in_specs=[hbm] * 3,
+            in_specs=[vmem] * 3,
             out_specs=[hbm] * 3,
             scratch_shapes=[pltpu.SemaphoreType.DMA((3,))],
-            compiler_params=pltpu.CompilerParams(vmem_limit_bytes=60 * 1024 * 1024),
+            compiler_params=pltpu.CompilerParams(vmem_limit_bytes=8 * 1024 * 1024),
         )(*done)
 
     in_specs = (P(None, None, "rows", "cols"), P(None, "rows", "cols"), P(), P(), P(), P())

time: 110 us -> 62 us (0.56)
  Pallas kernels: 110 us -> 61.2 us
    pallas_call x1, Pallas kernels: 48.8 us -> 1.17 us  [shards(): pl.pallas_call(write_out, out_shape=[jax.ShapeDtypeStruct(power.shape, f3...]
where the time goes in v2:
time: 62 us; the launch traced here: 61.9 us
  Pallas kernels  61.2 us (99%)
  between operations  0.64 us (1%)
    pallas_call x1, Pallas kernels, shards(): pl.pallas_call(body, out_shape=[pltpu.VMEM(power.shape, f32)] * 3, in_spe...  60.1 us

profile of v2, /device:TPU:12, one launch (start us, length us, event | category | flops | bytes accessed | tf_op | source)
XLA Modules:
  0.0 61.9 jit_solution(17173116802519021582)
XLA Ops:
  0.6 60.1 %shard_map.112 = (f32[2,4,128,128]{3,2,1,0:T(8,128)S(1)}, f32[2,4,128,128]{3,2,1,0:T(8,128)S(1)}, f32[2,4,128,128]{3,2,1,0:T(8,128)S(1)}) custom-call(f32[2,4,128,128]{3,2,1,0:T(8,128)} %refs_0_.1, s32[4,128,128]{2,1,0:T(8,128)} %refs_1_.1, bf16[3,256,256]{2,1,0:T(8,128)(2,1)} %constant.6.clone.refs_2_, bf16[3,256,256]{2,1,0:T(8,128)(2,1)} %constant.7.clone.refs_3_, ...), custom_call_target="tpu_custom_call" | custom-call | tf_op jit(solution)/shard_map/pallas_call | solution.py:541
  60.7 1.2 %shard_map.113 = (f32[2,4,128,128]{3,2,1,0:T(8,128)}, f32[2,4,128,128]{3,2,1,0:T(8,128)}, f32[2,4,128,128]{3,2,1,0:T(8,128)}) custom-call(f32[2,4,128,128]{3,2,1,0:T(8,128)S(1)} %get-tuple-element.6.refs_0_, f32[2,4,128,128]{3,2,1,0:T(8,128)S(1)} %get-tuple-element.7.refs_1_, f32[2,4,128,128]{3,2,1,0:T(8,128)S(1)} %get-tuple-element.8.refs_2_), custom_call_target="tpu_custom_call" | custom-call | tf_op jit(solution)/shard_map/pallas_call | solution.py:582

commit v3 on v2

--- a/solution.py
+++ b/solution.py
@@ -379,6 +379,12 @@
                 halos.append(start_halo(halo_of(apply, v), [pre[v, t] for t in range(TIERS)]))
         return halos
 
+    def keep_frame(v, t, frame):
+        frame_res[v, t] = frame
+        return frame
+
+    backs = solve_frames(0, forward, res, keep_frame)
+
     for copy, may_receive in cond_halo:
         receive(copy, may_receive)
     for t in range(TIERS):
@@ -388,11 +394,6 @@
             upward[t] = VERT_C * 0.5 * (conds[t] + conds[t + 1])
     sink[...] = SINK_C * conds[0]
 
-    def keep_frame(v, t, frame):
-        frame_res[v, t] = frame
-        return frame
-
-    backs = solve_frames(0, forward, res, keep_frame)
     coarse_state = gather_end(0, gather)
     halos = finish_apply(0, backs, coarse_of(coarse_state))
 

time: 62 us -> 60.9 us (0.982)
  Pallas kernels: 61.2 us -> 60.1 us
    pallas_call x1, Pallas kernels: 60.1 us -> 58.9 us  [shards(): pl.pallas_call(body, out_shape=[pltpu.VMEM(power.shape, f32)] * 3, in_spe...]
where the time goes in v3:
time: 60.9 us; the launch traced here: 60.8 us
  Pallas kernels  60.1 us (99%)
  between operations  0.64 us (1%)
    pallas_call x1, Pallas kernels, shards(): pl.pallas_call(body, out_shape=[pltpu.VMEM(power.shape, f32)] * 3, in_spe...  58.9 us

profile of v3, /device:TPU:12, one launch (start us, length us, event | category | flops | bytes accessed | tf_op | source)
XLA Modules:
  0.0 60.8 jit_solution(1849286992606140415)
XLA Ops:
  0.6 58.9 %shard_map.112 = (f32[2,4,128,128]{3,2,1,0:T(8,128)S(1)}, f32[2,4,128,128]{3,2,1,0:T(8,128)S(1)}, f32[2,4,128,128]{3,2,1,0:T(8,128)S(1)}) custom-call(f32[2,4,128,128]{3,2,1,0:T(8,128)} %refs_0_.1, s32[4,128,128]{2,1,0:T(8,128)} %refs_1_.1, bf16[3,256,256]{2,1,0:T(8,128)(2,1)} %constant.6.clone.refs_2_, bf16[3,256,256]{2,1,0:T(8,128)(2,1)} %constant.7.clone.refs_3_, ...), custom_call_target="tpu_custom_call" | custom-call | tf_op jit(solution)/shard_map/pallas_call | solution.py:542
  59.6 1.2 %shard_map.113 = (f32[2,4,128,128]{3,2,1,0:T(8,128)}, f32[2,4,128,128]{3,2,1,0:T(8,128)}, f32[2,4,128,128]{3,2,1,0:T(8,128)}) custom-call(f32[2,4,128,128]{3,2,1,0:T(8,128)S(1)} %get-tuple-element.6.refs_0_, f32[2,4,128,128]{3,2,1,0:T(8,128)S(1)} %get-tuple-element.7.refs_1_, f32[2,4,128,128]{3,2,1,0:T(8,128)S(1)} %get-tuple-element.8.refs_2_), custom_call_target="tpu_custom_call" | custom-call | tf_op jit(solution)/shard_map/pallas_call | solution.py:583
